TPU v7x, 512 devices: a whole 4x8x8 slice. The times are simulated.
512 devices in a mesh: section: 2 (over x_hi), row: 16 (over z, core), col: 16 (over y, x_lo).
Axes of the slice: x: 4 (x_hi: 2, x_lo: 2; x = x_hi * 2 + x_lo), y: 8, z: 8, core: 2. Of those that a mesh axis runs over, the one named last changes fastest.
Arguments:
- ends: bfloat16 [2, 512, 12288], P('section', 'col', 'row'), may hold values from -6 to 6
- weights: bfloat16 [2, 12288, 12288], P('section', 'row', 'col'), may hold values from -0.0546875 to 0.0546875
- routes: int32 [16, 16], P('row'), may hold values 0 or 1
Outputs:
- ends_out: bfloat16 [2, 512, 12288], P('section', 'col', 'row')
- weight_grads: bfloat16 [2, 12288, 12288], P('section', 'row', 'col')
All inputs are finite; a program needn't handle non-finite values. No bound on the sum of `routes` on one device may be relied on, other than what follows from the above.
Results may differ from a plain program's by a relative error of at most 0.038.
Values may be sent and summed in bfloat16 or wider, within the bound.
A program may use at most 64 MiB of HBM per device.

v0:
```python
import jax
import jax.numpy as jnp
from jax import lax
from jax.sharding import PartitionSpec as P


def passed_along(value, axis, steps):
    count = lax.axis_size(axis)
    initial, last = (max(0, -steps), min(count, count - steps))
    return lax.ppermute(value, axis, [(source, source + steps) for source in range(initial, last)])


def gelu_pair(pre_act):
    values, backward = jax.vjp(jax.nn.gelu, pre_act)
    return (values, backward(jnp.ones_like(pre_act))[0])


def contract_last(left, right):
    return lax.dot_general(
        left, right, (((1,), (1,)), ((), ())), preferred_element_type=jnp.float32
    )


def contract_first(left, right):
    return lax.dot_general(
        left, right, (((0,), (0,)), ((), ())), preferred_element_type=jnp.float32
    )


def gated(flag, compute, shape):
    return lax.cond(flag, compute, lambda: jnp.zeros(shape, jnp.float32))


def masked_total(route_row, pieces_back):
    flattened = pieces_back.reshape(pieces_back.shape[0], -1)
    summed_rows = jnp.dot(
        route_row.astype(jnp.bfloat16), flattened, preferred_element_type=jnp.float32
    )
    return summed_rows.reshape(pieces_back.shape[1:])


def shards(ends, weights, routes):
    local_in = ends[0]
    matrix = weights[0]
    route_row = routes[0]
    groups = lax.axis_size("row")
    tok_dev = local_in.shape[0]
    feat_width = local_in.shape[1]
    tokens = tok_dev * groups
    section_a = lax.axis_index("section") == 0
    section_b = jnp.logical_not(section_a)
    gathered = lax.all_gather(local_in, "col", axis=0, tiled=True)
    pre_first = lax.psum_scatter(
        gated(
            section_a,
            lambda: jnp.dot(gathered, matrix, preferred_element_type=jnp.float32),
            (tok_dev * lax.axis_size("row"), feat_width),
        ).astype(jnp.bfloat16),
        "row",
        scatter_dimension=0,
        tiled=True,
    ).astype(jnp.float32)
    hidden_full, slope_first = gelu_pair(pre_first)
    hidden = hidden_full.astype(jnp.bfloat16)
    route_weights = route_row.astype(jnp.bfloat16)[:, None, None]
    grouped = lax.all_to_all(
        route_weights * hidden[None], "row", split_axis=0, concat_axis=0, tiled=True
    )
    slot_blocks = passed_along(grouped, "section", 1)
    slot_rows = slot_blocks.reshape(tokens, feat_width)
    partial_second = gated(
        section_b, lambda: contract_last(slot_rows, matrix), (tokens, feat_width)
    )
    pre_second = lax.psum(partial_second.astype(jnp.bfloat16), "col").astype(jnp.float32)
    output_all, slope_second = gelu_pair(pre_second)
    own_block = lax.dynamic_slice_in_dim(output_all, lax.axis_index("col") * tok_dev, tok_dev, 0)
    result_second = own_block.astype(jnp.bfloat16)
    grad_out = (gathered.astype(jnp.float32) * slope_second).astype(jnp.bfloat16)
    grad_second = gated(
        section_b, lambda: contract_first(grad_out, slot_rows), (feat_width, feat_width)
    )
    group_terms = gated(
        section_b,
        lambda: jnp.dot(grad_out, matrix, preferred_element_type=jnp.float32),
        (tokens, feat_width),
    )
    group_terms = group_terms.astype(jnp.bfloat16).reshape(groups, tok_dev, feat_width)
    crossed = passed_along(group_terms, "section", -1)
    returned = lax.all_to_all(crossed, "row", split_axis=0, concat_axis=0, tiled=True)
    grad_hidden = masked_total(route_row, returned).astype(jnp.bfloat16)
    grad_pre = (grad_hidden.astype(jnp.float32) * slope_first).astype(jnp.bfloat16)
    grad_all = lax.all_gather(grad_pre, "row", axis=0, tiled=True)
    grad_first = gated(
        section_a, lambda: contract_first(gathered, grad_all), (feat_width, feat_width)
    )
    grad_inputs = lax.psum_scatter(
        gated(
            section_a,
            lambda: contract_last(grad_all, matrix),
            (tok_dev * lax.axis_size("col"), feat_width),
        ).astype(jnp.bfloat16),
        "col",
        scatter_dimension=0,
        tiled=True,
    )
    ends_out = jnp.where(section_a, grad_inputs, result_second)[None]
    weight_grads = jnp.where(section_a, grad_first, grad_second).astype(jnp.bfloat16)[None]
    return (ends_out, weight_grads)


def solution(mesh):
    placed = (P("section", "col", "row"), P("section", "row", "col"), P("row", None))
    return jax.shard_map(
        shards,
        mesh=mesh,
        in_specs=placed,
        out_specs=(P("section", "col", "row"), P("section", "row", "col")),
        check_vma=False,
    )
```

profile of v0, /device:TPU:4, one launch (start us, length us, event | category | flops | bytes accessed | tf_op | source)
XLA Modules:
  0.0 451.3 jit_solution(14114353959988139396)
XLA Ops:
  7.2 38.6 %all-gather = bf16[1,512,768]{2,1,0:T(8,128)(2,1)S(1)} all-gather(bf16[1,32,768]{2,1,0:T(8,128)(2,1)} %param.15), channel_id=2, replica_groups=mesh['section'=2,'row'=16,'col'=16] {'col'}, dimensions={1}, use_global_device_ids=true | all-gather | bytes 835584 | tf_op jit(solution)/shard_map/all_gather | solution.py:52
  45.9 0.9 copy-done
  46.9 62.3 %reduce-scatter.3.cloned.1.call-done = bf16[32,768]{1,0:T(8,128)(2,1)} async-done(((bf16[512,768]{1,0:T(8,128)(2,1)}), bf16[32,768]{1,0:T(8,128)(2,1)}) %reduce-scatter.3.cloned.1.call-update) | async-done | bytes 49168 | tf_op jit(solution)/shard_map/reduce_scatter | solution.py:53
  109.2 0.8 fusion.20
  110.1 26.2 %all_to_all.10 = bf16[16,32,768]{2,1,0:T(8,128)(2,1)S(1)} all-to-all(bf16[16,32,768]{2,1,0:T(8,128)(2,1)S(1)} %broadcast_multiply_fusion), channel_id=1, replica_groups=mesh['section'=2,'row'=16,'col'=16] {'row'}, dimensions={0} | all-to-all | bytes 1572864 | tf_op jit(solution)/shard_map/all_to_all | solution.py:66
  136.3 1.3 collective-permute-start
  137.6 22.6 %collective-permute-done = bf16[16,32,768]{2,1,0:T(8,128)(2,1)} collective-permute-done((bf16[16,32,768]{2,1,0:T(8,128)(2,1)S(1)}, bf16[16,32,768]{2,1,0:T(8,128)(2,1)}, u32[]{:S(2)}, u32[]{:S(2)}) %collective-permute-start) | collective-permute-done | bytes 786464 | tf_op jit(solution)/shard_map/ppermute | solution.py:10
  160.2 1.9 conditional.7
  160.2 1.9 fusion.28
  162.1 0.9 copy-done.1
  163.0 140.2 %all-reduce.2.cloned.1.call-done = bf16[512,768]{1,0:T(8,128)(2,1)} async-done(((bf16[512,768]{1,0:T(8,128)(2,1)}), bf16[512,768]{1,0:T(8,128)(2,1)}) %all-reduce.2.cloned.1.call-update) | async-done | bytes 786448 | tf_op jit(solution)/shard_map/psum | solution.py:74
  303.3 3.4 add_multiply_fusion
  307.5 2.9 collective-permute-start.1
  310.4 8.6 %collective-permute-done.1 = bf16[16,32,768]{2,1,0:T(8,128)(2,1)} collective-permute-done((bf16[16,32,768]{2,1,0:T(8,128)(2,1)S(1)}, bf16[16,32,768]{2,1,0:T(8,128)(2,1)}, u32[]{:S(2)}, u32[]{:S(2)}) %collective-permute-start.1) | collective-permute-done | bytes 786464 | tf_op jit(solution)/shard_map/ppermute | solution.py:10
  319.0 7.2 %all-to-all-start.1 = ((bf16[16,32,768]{2,1,0:T(8,128)(2,1)}), bf16[16,32,768]{2,1,0:T(8,128)(2,1)S(1)}, u32[]{:S(2)}, u32[]{:S(2)}) async-start(bf16[16,32,768]{2,1,0:T(8,128)(2,1)} %collective-permute-done.1), calls=%async_computation.2 | async-start | bytes 1572864 | tf_op jit(solution)/shard_map/all_to_all | solution.py:89
  326.3 20.6 %all-to-all-done.1 = bf16[16,32,768]{2,1,0:T(8,128)(2,1)S(1)} async-done(((bf16[16,32,768]{2,1,0:T(8,128)(2,1)}), bf16[16,32,768]{2,1,0:T(8,128)(2,1)S(1)}, u32[]{:S(2)}, u32[]{:S(2)}) %all-to-all-start.1) | async-done | bytes 786464 | tf_op jit(solution)/shard_map/all_to_all | solution.py:89
  347.5 20.1 %all_gather.7 = bf16[512,768]{1,0:T(8,128)(2,1)} all-gather(bf16[32,768]{1,0:T(8,128)(2,1)S(1)} %fusion.16), channel_id=1, replica_groups=mesh['section'=2,'row'=16,'col'=16] {'row'}, dimensions={0}, use_global_device_ids=true | all-gather | bytes 835584 | tf_op jit(solution)/shard_map/all_gather | solution.py:92
  367.7 0.9 copy-done.2
  368.6 2.0 conditional.11
  368.6 2.0 fusion.32
  370.7 1.2 convert_element_type.73
  372.1 1.1 fusion.8
  373.2 70.0 %reduce-scatter.5.cloned.1.call-done = bf16[32,768]{1,0:T(8,128)(2,1)} async-done(((bf16[512,768]{1,0:T(8,128)(2,1)}), bf16[32,768]{1,0:T(8,128)(2,1)}) %reduce-scatter.5.cloned.1.call-update) | async-done | bytes 49168 | tf_op jit(solution)/shard_map/reduce_scatter | solution.py:96
  443.2 1.6 fusion.24
  (33 shorter events, 3.0 us)
Async XLA Ops:
  7.2 102.0 %reduce-scatter.3.cloned.1.call-start = ((), (), s32[]{:S(2)}) async-start(), calls=%async_computation.4 | async-start | bytes 835584 | tf_op jit(solution)/shard_map/reduce_scatter | solution.py:53
  45.8 257.5 %copy-start.3 = (bf16[1,512,768]{2,1,0:T(8,128)(2,1)}, bf16[1,512,768]{2,1,0:T(8,128)(2,1)S(1)}, u32[]{:S(2)}) copy-start(bf16[1,512,768]{2,1,0:T(8,128)(2,1)S(1)} %all-gather) | copy-start | bytes 2359300
  45.8 1.1 copy-start.8
  45.9 0.9 copy-start
  45.9 114.3 %copy-start.7 = (bf16[1,768,768]{2,1,0:T(8,128)(2,1)S(1)}, bf16[1,768,768]{2,1,0:T(8,128)(2,1)}, u32[]{:S(2)}) copy-start(bf16[1,768,768]{2,1,0:T(8,128)(2,1)} %param.16) | copy-start | bytes 3538948
  46.8 256.4 %all-reduce.2.cloned.1.call-start = ((), (), s32[]{:S(2)}) async-start(), calls=%async_computation.5 | async-start | bytes 1572864 | tf_op jit(solution)/shard_map/psum | solution.py:74
  136.3 23.9 %collective-permute-start = (bf16[16,32,768]{2,1,0:T(8,128)(2,1)S(1)}, bf16[16,32,768]{2,1,0:T(8,128)(2,1)}, u32[]{:S(2)}, u32[]{:S(2)}) collective-permute-start(bf16[16,32,768]{2,1,0:T(8,128)(2,1)S(1)} %all_to_all.10), channel_id=1, source_target_pairs={{0,256},{1,257},{2,258},{3,259},{4,260},{5,261},{6,262},{7,263},{8... | collective-permute-start | bytes 2359304 | tf_op jit(solution)/shard_map/ppermute | solution.py:10
  162.1 0.9 copy-start.1
  307.5 39.9 %copy-start.6 = (bf16[32,768]{1,0:T(8,128)(2,1)S(1)}, bf16[32,768]{1,0:T(8,128)(2,1)}, u32[]{:S(2)}) copy-start(bf16[32,768]{1,0:T(8,128)(2,1)} %reduce-scatter.3.cloned.1.call-done) | copy-start | bytes 147460
  307.5 11.5 %collective-permute-start.1 = (bf16[16,32,768]{2,1,0:T(8,128)(2,1)S(1)}, bf16[16,32,768]{2,1,0:T(8,128)(2,1)}, u32[]{:S(2)}, u32[]{:S(2)}) collective-permute-start(bf16[16,32,768]{2,1,0:T(8,128)(2,1)S(1)} %bitcast.45), channel_id=1, source_target_pairs={{256,0},{257,1},{258,2},{259,3},{260,4},{261,5},{262,6},{263,7},{2... | collective-permute-start | bytes 2359304 | tf_op jit(solution)/shard_map/ppermute | solution.py:10
  319.0 27.9 %all-to-all-start.1 = ((bf16[16,32,768]{2,1,0:T(8,128)(2,1)}), bf16[16,32,768]{2,1,0:T(8,128)(2,1)S(1)}, u32[]{:S(2)}, u32[]{:S(2)}) async-start(bf16[16,32,768]{2,1,0:T(8,128)(2,1)} %collective-permute-done.1), calls=%async_computation.2 | async-start | bytes 1572864 | tf_op jit(solution)/shard_map/all_to_all | solution.py:89
  326.2 117.0 %reduce-scatter.5.cloned.1.call-start = ((), (), s32[]{:S(2)}) async-start(), calls=%async_computation.6 | async-start | bytes 835584 | tf_op jit(solution)/shard_map/reduce_scatter | solution.py:96
  367.7 0.9 copy-start.2
  368.6 2.1 copy-start.5
  370.6 1.3 copy-start.4
Sparse Core Ops, SparseCore 0:
  47.0 62.1 reduce-scatter.2
  163.2 140.0 all-reduce.1
  368.7 74.4 reduce-scatter.4
where the time goes:
time: 452 us; the launch traced here: 451 us
  waiting for transfers between devices  324 us (72%)
  blocking collectives  84.8 us (19%)
  between operations  13.9 us (3%)
  starting transfers between devices  11.5 us (3%)
  other arithmetic  8.43 us (2%)
  matrix products  5.25 us (1%)
    psum x1, waiting for transfers between devices, shards(): lax.psum(partial_second.astype(jnp.bfloat16), 'col').astype(jnp.float32)  140 us
    reduce_scatter x1, waiting for transfers between devices, shards(): lax.psum_scatter(gated(section_a, lambda: contract_last(grad_all, matrix)...  70 us
    reduce_scatter x1, waiting for transfers between devices, shards(): lax.psum_scatter(gated(section_a, lambda: jnp.dot(gathered, matrix, prefe...  62.3 us
    all_gather x1, blocking collectives, shards(): gathered = lax.all_gather(local_in, 'col', axis=0, tiled=True)  38.6 us
    ppermute x2, waiting for transfers between devices, passed_along(): lax.ppermute(value, axis, [(source, source + steps) for source in range(i...  31.2 us
    all_to_all x1, blocking collectives, shards(): lax.all_to_all(route_weights * hidden[None], 'row', split_axis=0, concat_...  26.2 us
    all_to_all x1, waiting for transfers between devices, shards(): lax.all_to_all(crossed, 'row', split_axis=0, concat_axis=0, tiled=True)  20.6 us
    all_gather x1, blocking collectives, shards(): grad_all = lax.all_gather(grad_pre, 'row', axis=0, tiled=True)  20.1 us
  transfers between devices with their start and end apart: 6, of which 6 were waited for; matrix products, arithmetic and copies ran while one was open for 1% of the time, Pallas kernels for 0%

commit v1 on v0

v1 whole, which is shorter than its diff:
```python
import functools
import math

import jax
import jax.numpy as jnp
from jax import lax
from jax.experimental import pallas as pl
from jax.experimental.pallas import tpu as pltpu
from jax.sharding import PartitionSpec as P

MESH = pl.DeviceIdType.MESH
HALVES = 2
ROWS = 16
TILE = 256
GELU_SCALE = math.sqrt(2.0 / math.pi)
GELU_CUBE = 0.044715


def gelu_pair(x):
    square = x * x
    t = jnp.tanh(GELU_SCALE * (x + GELU_CUBE * x * square))
    cdf = 0.5 * (1.0 + t)
    inner = GELU_SCALE * (1.0 + 3.0 * GELU_CUBE * square)
    return x * cdf, cdf + 0.5 * x * (1.0 - t * t) * inner


def rows_of(slot):
    return pl.ds(pl.multiple_of(slot * ROWS, ROWS), ROWS)


def offset_of(i, n):
    j = (i + 1) // 2
    return n // 2 + j * (1 - 2 * (i % 2))


class Line:
    def __init__(self, axis, n, place):
        self.n = n
        me = lax.axis_index(axis)
        self.pos = me // 2
        self.par = me % 2
        self.place = place

    def peer(self, pos):
        return self.place(pos * 2 + self.par)

    def sibling(self):
        return self.place(self.pos * 2 + 1 - self.par)

    def over_peers(self, body, near_first=False):
        def step(i, carry):
            k = self.n - 2 - i if near_first else i
            body(lax.rem(self.pos + offset_of(k, self.n), self.n))
            return carry

        lax.fori_loop(0, self.n - 1, step, 0)


def over(n, body):
    def step(i, carry):
        body(i)
        return carry

    lax.fori_loop(0, n, step, 0)


class Gather:
    def __init__(self, line, buf, ring_send, ring_recv, pair_send, pair_recv):
        self.line, self.buf = line, buf
        self.ring_send, self.ring_recv = ring_send, ring_recv
        self.pair_send, self.pair_recv = pair_send, pair_recv

    def own(self, h):
        line = self.line
        return self.buf.at[h, rows_of(line.par * line.n + line.pos)]

    def to_ring(self, h, pos):
        line = self.line
        return pltpu.make_async_remote_copy(
            src_ref=self.own(h), dst_ref=self.own(h),
            send_sem=self.ring_send.at[h, pos], recv_sem=self.ring_recv.at[h, line.pos],
            device_id=line.peer(pos), device_id_type=MESH)

    def from_ring(self, h, pos):
        line = self.line
        block = self.buf.at[h, rows_of(line.par * line.n + pos)]
        return pltpu.make_async_remote_copy(
            src_ref=block, dst_ref=block,
            send_sem=self.ring_send.at[h, pos], recv_sem=self.ring_recv.at[h, pos],
            device_id=line.peer(pos), device_id_type=MESH)

    def pair(self, h, par, pos):
        line = self.line
        block = self.buf.at[h, rows_of(par * line.n + pos)]
        return pltpu.make_async_remote_copy(
            src_ref=block, dst_ref=block,
            send_sem=self.pair_send.at[h, pos], recv_sem=self.pair_recv.at[h, pos],
            device_id=line.sibling(), device_id_type=MESH)

    def start(self, h):
        line = self.line
        line.over_peers(lambda pos: self.to_ring(h, pos).start())
        self.pair(h, line.par, line.pos).start()

    def finish(self, h):
        line = self.line

        def forward(pos):
            self.from_ring(h, pos).wait_recv()
            self.pair(h, line.par, pos).start()

        line.over_peers(forward, near_first=True)
        over(line.n, lambda pos: self.pair(h, 1 - line.par, pos).wait_recv())

    def drain(self, h):
        line = self.line
        line.over_peers(lambda pos: self.to_ring(h, pos).wait_send())
        over(line.n, lambda pos: self.pair(h, line.par, pos).wait_send())


class Scatter:
    def __init__(self, line, out, kept, got, both, land, pair_send, pair_recv, ring_send, ring_recv):
        self.line = line
        self.out, self.kept, self.got, self.both, self.land = out, kept, got, both, land
        self.pair_send, self.pair_recv = pair_send, pair_recv
        self.ring_send, self.ring_recv = ring_send, ring_recv

    def pair(self, h):
        return pltpu.make_async_remote_copy(
            src_ref=self.out.at[h], dst_ref=self.got.at[h],
            send_sem=self.pair_send.at[h], recv_sem=self.pair_recv.at[h],
            device_id=self.line.sibling(), device_id_type=MESH)

    def to_ring(self, h, pos):
        line = self.line
        return pltpu.make_async_remote_copy(
            src_ref=self.both.at[h, rows_of(pos)], dst_ref=self.land.at[h, rows_of(line.pos)],
            send_sem=self.ring_send.at[h, pos], recv_sem=self.ring_recv.at[h, line.pos],
            device_id=line.peer(pos), device_id_type=MESH)

    def from_ring(self, h, pos):
        line = self.line
        return pltpu.make_async_remote_copy(
            src_ref=self.both.at[h, rows_of(pos)], dst_ref=self.land.at[h, rows_of(pos)],
            send_sem=self.ring_send.at[h, pos], recv_sem=self.ring_recv.at[h, pos],
            device_id=line.peer(pos), device_id_type=MESH)

    def multiply(self, h, buf, w, transposed):
        line = self.line
        size = line.n * ROWS
        width = w.shape[0]
        tile = min(TILE, width)

        def product(par, store):
            left = buf[h, pl.ds(pl.multiple_of(par * size, size), size), :]

            def column(j):
                cut = pl.ds(pl.multiple_of(j * tile, tile), tile)
                if transposed:
                    store(cut, lax.dot_general(
                        left, w[cut, :], (((1,), (1,)), ((), ())), preferred_element_type=jnp.float32))
                else:
                    store(cut, jnp.dot(left, w[:, cut], preferred_element_type=jnp.float32))

            over(width // tile, column)

        def to_out(cut, value):
            self.out[h, :, cut] = value.astype(jnp.bfloat16)

        def to_kept(cut, value):
            self.kept[h, :, cut] = value

        product(1 - line.par, to_out)
        self.pair(h).start()
        product(line.par, to_kept)

    def combine(self, h):
        line = self.line
        self.pair(h).wait_recv()
        self.both[h] = (self.kept[h] + self.got[h].astype(jnp.float32)).astype(jnp.bfloat16)
        line.over_peers(lambda pos: self.to_ring(h, pos).start())

    def finish(self, h):
        line = self.line
        line.over_peers(lambda pos: self.from_ring(h, pos).wait_recv(), near_first=True)
        own = self.both[h, rows_of(line.pos), :]
        self.land[h, rows_of(line.pos), :] = own
        total = self.land[h, pl.ds(0, ROWS), :].astype(jnp.float32)
        for pos in range(1, line.n):
            total = total + self.land[h, pl.ds(pos * ROWS, ROWS), :].astype(jnp.float32)
        return total

    def drain(self, h):
        line = self.line
        self.pair(h).wait_send()
        line.over_peers(lambda pos: self.to_ring(h, pos).wait_send())


def kernel(n, ends_ref, w_hbm, routes_ref, ends_out, dw_hbm,
           w, col_buf, row_buf, dy, outgoing, incoming, slope, route_tiles, dw,
           rs_out, rs_kept, rs_got, rs_both, rs_land,
           ag_ring_send, ag_ring_recv, ag_pair_send, ag_pair_recv,
           rs_ring_send, rs_ring_recv, rs_pair_send, rs_pair_recv,
           cross_send, cross_recv, rt_send, rt_recv, rt_pair_send, rt_pair_recv, local_sem):
    s, r, c = lax.axis_index("section"), lax.axis_index("row"), lax.axis_index("col")
    row = Line("row", n, lambda i: (s, i, c))
    col = Line("col", n, lambda i: (s, r, i))
    over_there = (1 - s, r, c)

    ag_col = Gather(col, col_buf, ag_ring_send.at[0], ag_ring_recv.at[0], ag_pair_send.at[0], ag_pair_recv.at[0])
    ag_row = Gather(row, row_buf, ag_ring_send.at[1], ag_ring_recv.at[1], ag_pair_send.at[1], ag_pair_recv.at[1])

    def scatter(line, k):
        return Scatter(line, rs_out.at[k], rs_kept.at[k], rs_got.at[k], rs_both.at[k], rs_land.at[k],
                       rs_pair_send.at[k], rs_pair_recv.at[k], rs_ring_send.at[k], rs_ring_recv.at[k])

    rs_row, rs_col = scatter(row, 0), scatter(col, 1)

    def cross(h, dst):
        return pltpu.make_async_remote_copy(
            src_ref=outgoing.at[h], dst_ref=dst,
            send_sem=cross_send.at[h], recv_sem=cross_recv.at[h],
            device_id=over_there, device_id_type=MESH)

    load_w = pltpu.make_async_copy(w_hbm.at[0], w, local_sem.at[0])
    store_dw = pltpu.make_async_copy(dw, dw_hbm.at[0], local_sem.at[1])
    load_w.start()

    barrier = pltpu.get_barrier_semaphore()

    def greet(device):
        pl.semaphore_signal(barrier, inc=1, device_id=device, device_id_type=MESH)

    col.over_peers(lambda pos: greet(col.peer(pos)))
    greet(col.sibling())
    row.over_peers(lambda pos: greet(row.peer(pos)))
    greet(row.sibling())
    greet(over_there)

    def load_ends(h, dst):
        return pltpu.make_async_copy(ends_ref.at[0, pl.ds(h * ROWS, ROWS)], dst, local_sem.at[2 + h])

    def weight_grad():
        width = w.shape[0]
        tile = min(TILE, width)

        def block(k):
            at_row = pl.ds(pl.multiple_of((k // (width // tile)) * tile, tile), tile)
            at_col = pl.ds(pl.multiple_of((k % (width // tile)) * tile, tile), tile)
            total = jnp.zeros((tile, tile), jnp.float32)
            for h in range(HALVES):
                total = total + lax.dot_general(
                    col_buf[h, :, at_row], row_buf[h, :, at_col], (((0,), (0,)), ((), ())),
                    preferred_element_type=jnp.float32)
            dw[at_row, at_col] = total.astype(jnp.bfloat16)

        over((width // tile) ** 2, block)
        store_dw.start()

    def col_to_row():
        for h in range(HALVES):
            ag_col.finish(h)
            if h == 0:
                pl.when(s == 0)(load_w.wait)
            rs_row.multiply(h, col_buf, w, False)
            rs_row.combine(h)

    def row_to_col():
        for h in range(HALVES):
            ag_row.finish(h)
            if h == 0:
                pl.when(s == 1)(load_w.wait)
            rs_col.multiply(h, row_buf, w, True)
        for h in range(HALVES):
            rs_col.combine(h)

    halves = range(HALVES)

    @pl.when(s == 0)
    def _():
        for h in halves:
            load_ends(h, ag_col.own(h)).start()
        for h in halves:
            load_ends(h, ag_col.own(h)).wait()
        pl.semaphore_wait(barrier, 2 * (n - 1) + 3)
        for h in halves:
            ag_col.start(h)
        col_to_row()
        for h in halves:
            value, grad = gelu_pair(rs_row.finish(h))
            outgoing[h] = value.astype(jnp.bfloat16)
            cross(h, ag_row.own(h)).start()
            slope[h] = grad
        for h in halves:
            ag_col.drain(h)
            rs_row.drain(h)
        for h in halves:
            cross(h, incoming.at[h]).wait_recv()
            grad = incoming[h].astype(jnp.float32) * slope[h]
            ag_row.own(h)[...] = grad.astype(jnp.bfloat16)
            ag_row.start(h)
        row_to_col()
        weight_grad()
        for h in halves:
            ends_out[0, pl.ds(h * ROWS, ROWS), :] = rs_col.finish(h).astype(jnp.bfloat16)
        for h in halves:
            cross(h, ag_row.own(h)).wait_send()
            ag_row.drain(h)
            rs_col.drain(h)
        store_dw.wait()

    @pl.when(s == 1)
    def _():
        for h in halves:
            load_ends(h, dy.at[h]).start()
        route_tiles[row.par, row.pos] = jnp.zeros((8, 128), jnp.float32)
        route_tiles[row.par, row.pos, 0:1, 0:2 * n] = routes_ref[...].astype(jnp.float32)
        for h in halves:
            load_ends(h, dy.at[h]).wait()
        pl.semaphore_wait(barrier, 2 * (n - 1) + 3)

        def tile_to(pos):
            mine = route_tiles.at[row.par, row.pos]
            return pltpu.make_async_remote_copy(
                src_ref=mine, dst_ref=mine, send_sem=rt_send.at[pos], recv_sem=rt_recv.at[row.pos],
                device_id=row.peer(pos), device_id_type=MESH)

        def tile_from(pos):
            tile = route_tiles.at[row.par, pos]
            return pltpu.make_async_remote_copy(
                src_ref=tile, dst_ref=tile, send_sem=rt_send.at[pos], recv_sem=rt_recv.at[pos],
                device_id=row.peer(pos), device_id_type=MESH)

        def tiles(par):
            return pltpu.make_async_remote_copy(
                src_ref=route_tiles.at[par], dst_ref=route_tiles.at[par],
                send_sem=rt_pair_send.at[0], recv_sem=rt_pair_recv.at[0],
                device_id=row.sibling(), device_id_type=MESH)

        row.over_peers(lambda pos: tile_to(pos).start())
        row.over_peers(lambda pos: tile_from(pos).wait_recv())
        tiles(row.par).start()
        tiles(1 - row.par).wait_recv()
        row.over_peers(lambda pos: tile_to(pos).wait_send())
        tiles(row.par).wait_send()
        picked = route_tiles[col.par, col.pos, 0:1, :]
        lanes = lax.broadcasted_iota(jnp.int32, (1, 128), 1)
        routed = jnp.sum(jnp.where(lanes == r, picked, 0.0), axis=1, keepdims=True)

        for h in halves:
            cross(h, ag_row.own(h)).wait_recv()
            ag_row.start(h)
        row_to_col()
        for h in halves:
            value, grad = gelu_pair(rs_col.finish(h) * routed)
            masked = (dy[h].astype(jnp.float32) * grad).astype(jnp.bfloat16).astype(jnp.float32) * routed
            ag_col.own(h)[...] = masked.astype(jnp.bfloat16)
            ag_col.start(h)
            ends_out[0, pl.ds(h * ROWS, ROWS), :] = value.astype(jnp.bfloat16)
        col_to_row()
        for h in halves:
            outgoing[h] = rs_row.finish(h).astype(jnp.bfloat16)
            cross(h, incoming.at[h]).start()
        weight_grad()
        for h in halves:
            ag_col.drain(h)
            rs_row.drain(h)
            ag_row.drain(h)
            rs_col.drain(h)
            cross(h, incoming.at[h]).wait_send()
        store_dw.wait()


def shards(ends, weights, routes):
    width = weights.shape[1]
    n = lax.axis_size("row") // 2
    half = n * ROWS
    bf16, f32 = jnp.bfloat16, jnp.float32
    dma = pltpu.SemaphoreType.DMA
    anywhere = pl.BlockSpec(memory_space=pl.ANY)
    in_vmem = pl.BlockSpec(memory_space=pltpu.VMEM)
    return pl.pallas_call(
        functools.partial(kernel, n),
        out_shape=(jax.ShapeDtypeStruct(ends.shape, bf16), jax.ShapeDtypeStruct(weights.shape, bf16)),
        in_specs=[anywhere, anywhere, in_vmem],
        out_specs=(in_vmem, anywhere),
        scratch_shapes=[
            pltpu.VMEM((width, width), bf16),
            pltpu.VMEM((HALVES, 2 * half, width), bf16),
            pltpu.VMEM((HALVES, 2 * half, width), bf16),
            pltpu.VMEM((HALVES, ROWS, width), bf16),
            pltpu.VMEM((HALVES, ROWS, width), bf16),
            pltpu.VMEM((HALVES, ROWS, width), bf16),
            pltpu.VMEM((HALVES, ROWS, width), f32),
            pltpu.VMEM((2, n, 8, 128), f32),
            pltpu.VMEM((width, width), bf16),
            pltpu.VMEM((2, HALVES, half, width), bf16),
            pltpu.VMEM((2, HALVES, half, width), f32),
            pltpu.VMEM((2, HALVES, half, width), bf16),
            pltpu.VMEM((2, HALVES, half, width), bf16),
            pltpu.VMEM((2, HALVES, half, width), bf16),
            dma((2, HALVES, n)), dma((2, HALVES, n)), dma((2, HALVES, n)), dma((2, HALVES, n)),
            dma((2, HALVES, n)), dma((2, HALVES, n)), dma((2, HALVES)), dma((2, HALVES)),
            dma((HALVES,)), dma((HALVES,)), dma((n,)), dma((n,)), dma((1,)), dma((1,)), dma((4,)),
        ],
        compiler_params=pltpu.CompilerParams(
            collective_id=0, has_side_effects=True, vmem_limit_bytes=40 * 2**20),
        cost_estimate=pl.CostEstimate(
            flops=6 * half * 4 * width * width, bytes_accessed=4 * width * width, transcendentals=0),
    )(ends, weights, routes)


def solution(mesh):
    placed = (P("section", "col", "row"), P("section", "row", "col"), P("row", None))
    return jax.shard_map(
        shards,
        mesh=mesh,
        in_specs=placed,
        out_specs=(P("section", "col", "row"), P("section", "row", "col")),
        check_vma=False,
    )
```

time: 452 us -> 126 us (0.28)
  the two profiles are of different devices: /device:TPU:4 before, /device:TPU:1 now
where the time goes in v1:
time: 126 us; the launch traced here: 125 us
  Pallas kernels  120 us (95%)
  local copies, waits for them, and re-layouts  4.35 us (3%)
    pallas_call x1, Pallas kernels, shards(): pl.pallas_call(functools.partial(kernel, n), out_shape=(jax.ShapeDtypeStr...  120 us
    unnamed x8, local copies, waits for them, and re-layouts  4.35 us

profile of v1, /device:TPU:1, one launch (start us, length us, event | category | flops | bytes accessed | tf_op | source)
XLA Modules:
  0.0 125.3 jit_solution(980641197241397603)
XLA Ops:
  0.6 0.0 copy-start
  0.6 1.3 %copy-done = bf16[1,768,768]{2,1,0:T(8,128)(2,1)S(1)} copy-done((bf16[1,768,768]{2,1,0:T(8,128)(2,1)S(1)}, bf16[1,768,768]{2,1,0:T(8,128)(2,1)}, u32[]{:S(2)}) %copy-start) | copy-done | bytes 1179672
  1.9 0.0 copy-start.1
  1.9 0.8 copy-done.1
  2.7 0.0 copy-start.2
  2.7 0.7 copy-done.2
  3.4 120.3 %shard_map.50 = (bf16[1,32,768]{2,1,0:T(8,128)(2,1)S(1)}, bf16[1,768,768]{2,1,0:T(8,128)(2,1)S(1)}) custom-call(bf16[1,32,768]{2,1,0:T(8,128)(2,1)S(1)} %copy-done.1, bf16[1,768,768]{2,1,0:T(8,128)(2,1)S(1)} %copy-done, s32[1,16]{1,0:T(1,128)S(1)} %copy-done.2), custom_call_target="tpu_custom_call" | custom-call | flops 1811939328 | bytes 2359296 | tf_op jit(solution)/shard_map/pallas_call | solution.py:382
  123.7 0.6 copy.7
  124.3 1.0 copy.8
Async XLA Ops:
  0.6 1.3 %copy-start = (bf16[1,768,768]{2,1,0:T(8,128)(2,1)S(1)}, bf16[1,768,768]{2,1,0:T(8,128)(2,1)}, u32[]{:S(2)}) copy-start(bf16[1,768,768]{2,1,0:T(8,128)(2,1)} %w_hbm.1) | copy-start | bytes 3538948
  1.9 0.8 copy-start.1
  2.7 0.7 copy-start.2

commit v2 on v1

v2 whole, which is shorter than its diff:
```python
import functools
import math

import jax
import jax.numpy as jnp
from jax import lax
from jax.experimental import pallas as pl
from jax.experimental.pallas import tpu as pltpu
from jax.sharding import PartitionSpec as P

MESH = pl.DeviceIdType.MESH
HALVES = 2
ROWS = 16
TILE = 256
FAR_GATHER = 0
FAR_SUM = 0
FAR_CROSS = 0
WHOLE_ROW_PAIR = True
VMEM_LIMIT = 62 * 2**20
GELU_SCALE = math.sqrt(2.0 / math.pi)
GELU_CUBE = 0.044715


def gelu_pair(x):
    square = x * x
    t = jnp.tanh(GELU_SCALE * (x + GELU_CUBE * x * square))
    cdf = 0.5 * (1.0 + t)
    inner = GELU_SCALE * (1.0 + 3.0 * GELU_CUBE * square)
    return x * cdf, cdf + 0.5 * x * (1.0 - t * t) * inner


def rows_of(slot):
    return pl.ds(pl.multiple_of(slot * ROWS, ROWS), ROWS)


def over(first, last, body):
    def step(i, carry):
        body(i)
        return carry

    if first < last:
        lax.fori_loop(first, last, step, 0)


def remote(src, dst, send_sem, recv_sem, device):
    return pltpu.make_async_remote_copy(
        src_ref=src, dst_ref=dst, send_sem=send_sem, recv_sem=recv_sem,
        device_id=device, device_id_type=MESH)


class Line:
    def __init__(self, axis, n, place):
        self.n = n
        me = lax.axis_index(axis)
        self.pos = me // 2
        self.par = me % 2
        self.place = place

    def peer(self, pos):
        return self.place(pos * 2 + self.par)

    def other(self, pos):
        return self.place(pos * 2 + 1 - self.par)

    def at(self, i):
        j = (i + 1) // 2
        return lax.rem(self.pos + self.n // 2 + j * (1 - 2 * (i % 2)) + self.n, self.n)

    def peers(self, first, last, body):
        over(first, last, lambda i: body(self.at(i)))

    def peers_back(self, first, last, body):
        over(first, last, lambda i: body(self.at(first + last - 1 - i)))


class Gather:
    def __init__(self, line, buf, skip, far, ring_send, ring_recv, pair_send, pair_recv, far_send):
        self.line, self.buf, self.skip, self.far = line, buf, skip, far
        self.ring_send, self.ring_recv = ring_send, ring_recv
        self.pair_send, self.pair_recv = pair_send, pair_recv
        self.far_send = far_send

    def own(self, h):
        line = self.line
        return self.buf.at[h, rows_of(line.par * line.n + line.pos)]

    def ring(self, h, block_pos, peer_pos):
        line = self.line
        block = self.buf.at[h, rows_of(line.par * line.n + block_pos)]
        return remote(block, block, self.ring_send.at[h, peer_pos], self.ring_recv.at[h, block_pos], line.peer(peer_pos))

    def to_ring(self, h, pos):
        return self.ring(h, self.line.pos, pos)

    def from_ring(self, h, pos):
        return self.ring(h, pos, pos)

    def to_far(self, h, pos):
        line = self.line
        return remote(self.own(h), self.own(h), self.far_send.at[h, pos], self.pair_recv.at[h, line.pos], line.other(pos))

    def pair(self, h, par, pos):
        line = self.line
        block = self.buf.at[h, rows_of(par * line.n + pos)]
        return remote(block, block, self.pair_send.at[h, pos], self.pair_recv.at[h, pos], line.other(line.pos))

    def start(self, h):
        line = self.line

        def both(pos):
            self.to_ring(h, pos).start()
            self.to_far(h, pos).start()

        line.peers(self.skip, self.far, both)
        line.peers(max(self.skip, self.far), line.n - 1, lambda pos: self.to_ring(h, pos).start())
        self.pair(h, line.par, line.pos).start()

    def finish_ring(self, h):
        line = self.line

        def forward(pos):
            self.from_ring(h, pos).wait_recv()
            self.pair(h, line.par, pos).start()

        line.peers_back(self.far, line.n - 1, forward)
        line.peers_back(0, self.far, lambda pos: self.from_ring(h, pos).wait_recv())

    def finish_pair(self, h):
        line = self.line
        over(0, line.n, lambda pos: self.pair(h, 1 - line.par, pos).wait_recv())

    def drain(self, h):
        line = self.line
        line.peers(self.skip, line.n - 1, lambda pos: self.to_ring(h, pos).wait_send())
        line.peers(self.skip, self.far, lambda pos: self.to_far(h, pos).wait_send())
        line.peers(self.far, line.n - 1, lambda pos: self.pair(h, line.par, pos).wait_send())
        self.pair(h, line.par, line.pos).wait_send()


class Scatter:
    def __init__(self, line, far, whole, out, kept, got, both, land, far_land,
                 pair_send, pair_recv, ring_send, ring_recv, far_send, far_recv):
        self.line, self.far, self.whole = line, far, whole
        self.out, self.kept, self.got, self.both = out, kept, got, both
        self.land, self.far_land = land, far_land
        self.pair_send, self.pair_recv = pair_send, pair_recv
        self.ring_send, self.ring_recv = ring_send, ring_recv
        self.far_send, self.far_recv = far_send, far_recv

    def pair(self, h, pos):
        line = self.line
        if self.whole:
            return remote(self.out.at[h, 1 - line.par], self.got.at[h], self.pair_send.at[h, 0], self.pair_recv.at[h, 0], line.other(line.pos))
        return remote(self.out.at[h, 1 - line.par, rows_of(pos)], self.got.at[h, rows_of(pos)],
                      self.pair_send.at[h, pos], self.pair_recv.at[h, pos], line.other(line.pos))

    def ring(self, h, pos, land_pos):
        return remote(self.both.at[h, rows_of(pos)], self.land.at[h, rows_of(land_pos)],
                      self.ring_send.at[h, pos], self.ring_recv.at[h, land_pos], self.line.peer(pos))

    def to_ring(self, h, pos):
        return self.ring(h, pos, self.line.pos)

    def from_ring(self, h, pos):
        return self.ring(h, pos, pos)

    def direct(self, h, pos, land_pos):
        return remote(self.out.at[h, 1 - self.line.par, rows_of(pos)], self.far_land.at[h, rows_of(land_pos)],
                      self.far_send.at[h, pos], self.far_recv.at[h, land_pos], self.line.other(pos))

    def to_far(self, h, pos):
        return self.direct(h, pos, self.line.pos)

    def from_far(self, h, pos):
        return self.direct(h, pos, pos)

    def multiply(self, h, buf, w, transposed, par):
        size = self.line.n * ROWS
        width = w.shape[0]
        tile = min(TILE, width)
        left = buf[h, pl.ds(pl.multiple_of(par * size, size), size), :]

        def column(j):
            cut = pl.ds(pl.multiple_of(j * tile, tile), tile)
            if transposed:
                value = lax.dot_general(left, w[cut, :], (((1,), (1,)), ((), ())), preferred_element_type=jnp.float32)
            else:
                value = jnp.dot(left, w[:, cut], preferred_element_type=jnp.float32)
            self.kept[h, par, :, cut] = value
            self.out[h, par, :, cut] = value.astype(jnp.bfloat16)

        over(0, width // tile, column)

    def send_pair(self, h):
        line = self.line
        line.peers(0, self.far, lambda pos: self.to_far(h, pos).start())
        if not self.whole:
            line.peers(self.far, line.n - 1, lambda pos: self.pair(h, pos).start())
        self.pair(h, line.pos).start()

    def send_far(self, h):
        line = self.line

        def send(pos):
            self.both[h, rows_of(pos), :] = self.out[h, line.par, rows_of(pos), :]
            self.to_ring(h, pos).start()

        line.peers(0, self.far, send)

    def combine(self, h):
        line = self.line
        if self.whole:
            self.pair(h, 0).wait_recv()

        def send(pos):
            if not self.whole:
                self.pair(h, pos).wait_recv()
            total = self.kept[h, line.par, rows_of(pos), :] + self.got[h, rows_of(pos), :].astype(jnp.float32)
            self.both[h, rows_of(pos), :] = total.astype(jnp.bfloat16)
            self.to_ring(h, pos).start()

        line.peers(self.far, line.n - 1, send)

    def finish(self, h):
        line = self.line
        if not self.whole:
            self.pair(h, line.pos).wait_recv()
        total = self.kept[h, line.par, rows_of(line.pos), :] + self.got[h, rows_of(line.pos), :].astype(jnp.float32)

        def near(i, total):
            pos = line.at(line.n - 2 - i)
            self.from_ring(h, pos).wait_recv()
            return total + self.land[h, rows_of(pos), :].astype(jnp.float32)

        total = lax.fori_loop(0, line.n - 1, near, total)

        def far(i, total):
            pos = line.at(self.far - 1 - i)
            self.from_far(h, pos).wait_recv()
            return total + self.far_land[h, rows_of(pos), :].astype(jnp.float32)

        return lax.fori_loop(0, self.far, far, total) if self.far else total

    def drain(self, h):
        line = self.line
        if not self.whole:
            line.peers(self.far, line.n - 1, lambda pos: self.pair(h, pos).wait_send())
        self.pair(h, line.pos).wait_send()
        line.peers(0, line.n - 1, lambda pos: self.to_ring(h, pos).wait_send())
        line.peers(0, self.far, lambda pos: self.to_far(h, pos).wait_send())


def kernel(n, ends_hbm, w_hbm, routes_hbm, ends_out, dw_hbm,
           w, col_buf, row_buf, dy, outgoing, slope, route_row, route_tiles, dw,
           rs_out, rs_kept, rs_got, rs_both, rs_land, rs_far_land,
           ag_ring_send, ag_ring_recv, ag_pair_send, ag_pair_recv, ag_far_send,
           rs_ring_send, rs_ring_recv, rs_pair_send, rs_pair_recv, rs_far_send, rs_far_recv,
           cross_send, cross_recv, cross_far_send, slope_send, slope_recv,
           rt_send, rt_recv, rt_pair_send, rt_pair_recv, local_sem):
    s, r, c = lax.axis_index("section"), lax.axis_index("row"), lax.axis_index("col")
    row = Line("row", n, lambda i: (s, i, c))
    col = Line("col", n, lambda i: (s, r, i))
    over_there = (1 - s, r, c)
    far_gather, far_sum, far_cross = (min(far, n - 1) for far in (FAR_GATHER, FAR_SUM, FAR_CROSS))
    halves = range(HALVES)

    def gather(line, buf, skip, far, k):
        return Gather(line, buf, skip, far, ag_ring_send.at[k], ag_ring_recv.at[k],
                      ag_pair_send.at[k], ag_pair_recv.at[k], ag_far_send.at[k])

    ag_col = gather(col, col_buf, 0, far_gather, 0)
    ag_row = gather(row, row_buf, far_cross, 0, 1)

    def scatter(line, far, whole, k):
        return Scatter(line, far, whole, rs_out.at[k], rs_kept.at[k], rs_got.at[k], rs_both.at[k],
                       rs_land.at[k], rs_far_land, rs_pair_send.at[k], rs_pair_recv.at[k],
                       rs_ring_send.at[k], rs_ring_recv.at[k], rs_far_send, rs_far_recv)

    rs_row, rs_col = scatter(row, 0, WHOLE_ROW_PAIR, 0), scatter(col, far_sum, False, 1)

    def cross(h):
        return remote(outgoing.at[h], ag_row.own(h), cross_send.at[h], cross_recv.at[h], over_there)

    def cross_far(h, pos):
        return remote(outgoing.at[h], ag_row.own(h), cross_far_send.at[h, pos],
                      ag_row.ring_recv.at[h, row.pos], (1 - s, pos * 2 + row.par, c))

    def cross_slope(h):
        return remote(slope.at[h], slope.at[h], slope_send.at[h], slope_recv.at[h], over_there)

    def cross_start(h):
        cross(h).start()
        row.peers(0, far_cross, lambda pos: cross_far(h, pos).start())

    def cross_drain(h):
        cross(h).wait_send()
        row.peers(0, far_cross, lambda pos: cross_far(h, pos).wait_send())

    load_w = pltpu.make_async_copy(w_hbm.at[0], w, local_sem.at[0])
    store_dw = pltpu.make_async_copy(dw, dw_hbm.at[0], local_sem.at[1])
    load_routes = pltpu.make_async_copy(routes_hbm, route_row, local_sem.at[4])

    def load_ends(h, dst):
        return pltpu.make_async_copy(ends_hbm.at[0, pl.ds(h * ROWS, ROWS)], dst, local_sem.at[2 + h])

    barrier = pltpu.get_barrier_semaphore()

    def greet(device):
        pl.semaphore_signal(barrier, inc=1, device_id=device, device_id_type=MESH)

    far_col = max(far_gather, far_sum)
    col.peers(0, n - 1, lambda pos: greet(col.peer(pos)))
    col.peers(0, far_col, lambda pos: greet(col.other(pos)))
    greet(col.other(col.pos))
    row.peers(0, n - 1, lambda pos: greet(row.peer(pos)))
    greet(row.other(row.pos))
    greet(over_there)
    row.peers(0, far_cross, lambda pos: greet((1 - s, pos * 2 + row.par, c)))
    greetings = 2 * (n - 1) + 3 + far_col + far_cross

    def weight_grad():
        width = w.shape[0]
        tile = min(TILE, width)

        def block(k):
            at_row = pl.ds(pl.multiple_of((k // (width // tile)) * tile, tile), tile)
            at_col = pl.ds(pl.multiple_of((k % (width // tile)) * tile, tile), tile)
            total = jnp.zeros((tile, tile), jnp.float32)
            for h in halves:
                total = total + lax.dot_general(
                    col_buf[h, :, at_row], row_buf[h, :, at_col], (((0,), (0,)), ((), ())),
                    preferred_element_type=jnp.float32)
            dw[at_row, at_col] = total.astype(jnp.bfloat16)

        over(0, (width // tile) ** 2, block)
        store_dw.start()

    same = row.par == col.par
    differ = row.par != col.par

    def col_to_row():
        for h in halves:
            ag_col.finish_ring(h)
            if h == 0:
                pl.when(s == 0)(load_w.wait)
            rs_row.multiply(h, col_buf, w, False, col.par)
            pl.when(differ)(lambda: rs_row.send_pair(h))
            pl.when(same)(lambda: rs_row.combine(h))
        for h in halves:
            ag_col.finish_pair(h)
            rs_row.multiply(h, col_buf, w, False, 1 - col.par)
            pl.when(same)(lambda: rs_row.send_pair(h))
            pl.when(differ)(lambda: rs_row.combine(h))

    def row_to_col():
        for h in halves:
            ag_row.finish_ring(h)
            if h == 0:
                pl.when(s == 1)(load_w.wait)
            rs_col.multiply(h, row_buf, w, True, row.par)
            pl.when(differ)(lambda: rs_col.send_pair(h))
            pl.when(same)(lambda: rs_col.send_far(h))
            ag_row.finish_pair(h)
            rs_col.multiply(h, row_buf, w, True, 1 - row.par)
            pl.when(same)(lambda: rs_col.send_pair(h))
            pl.when(differ)(lambda: rs_col.send_far(h))
        for h in halves:
            rs_col.combine(h)

    @pl.when(s == 0)
    def _():
        for h in halves:
            load_ends(h, ag_col.own(h)).start()
        load_w.start()
        for h in halves:
            load_ends(h, ag_col.own(h)).wait()
        pl.semaphore_wait(barrier, greetings)
        for h in halves:
            ag_col.start(h)
        col_to_row()
        for h in halves:
            value, grad = gelu_pair(rs_row.finish(h))
            outgoing[h] = value.astype(jnp.bfloat16)
            cross_start(h)
            slope[h] = grad
            cross_slope(h).start()
        for h in halves:
            ag_col.drain(h)
            rs_row.drain(h)
            cross_drain(h)
            cross_slope(h).wait_send()
        for h in halves:
            cross(h).wait_recv()
            ag_row.start(h)
        row_to_col()
        weight_grad()
        for h in halves:
            ends_out[0, pl.ds(h * ROWS, ROWS), :] = rs_col.finish(h).astype(jnp.bfloat16)
        for h in halves:
            ag_row.drain(h)
            rs_col.drain(h)
        store_dw.wait()

    @pl.when(s == 1)
    def _():
        load_routes.start()
        for h in halves:
            load_ends(h, dy.at[h]).start()
        load_w.start()
        load_routes.wait()
        route_tiles[row.par, row.pos] = jnp.zeros((8, 128), jnp.float32)
        route_tiles[row.par, row.pos, 0:1, 0:2 * n] = route_row[...].astype(jnp.float32)
        for h in halves:
            load_ends(h, dy.at[h]).wait()
        pl.semaphore_wait(barrier, greetings)

        def tile_to(pos):
            mine = route_tiles.at[row.par, row.pos]
            return remote(mine, mine, rt_send.at[pos], rt_recv.at[row.pos], row.peer(pos))

        def tile_from(pos):
            tile = route_tiles.at[row.par, pos]
            return remote(tile, tile, rt_send.at[pos], rt_recv.at[pos], row.peer(pos))

        def tiles(par):
            return remote(route_tiles.at[par], route_tiles.at[par], rt_pair_send.at[0], rt_pair_recv.at[0], row.other(row.pos))

        row.peers(0, n - 1, lambda pos: tile_to(pos).start())
        row.peers(0, n - 1, lambda pos: tile_from(pos).wait_recv())
        tiles(row.par).start()
        tiles(1 - row.par).wait_recv()
        row.peers(0, n - 1, lambda pos: tile_to(pos).wait_send())
        tiles(row.par).wait_send()
        picked = route_tiles[col.par, col.pos, 0:1, :]
        lanes = lax.broadcasted_iota(jnp.int32, (1, 128), 1)
        routed = jnp.sum(jnp.where(lanes == r, picked, 0.0), axis=1, keepdims=True)

        for h in halves:
            cross(h).wait_recv()
            ag_row.start(h)
        row_to_col()
        for h in halves:
            value, grad = gelu_pair(rs_col.finish(h) * routed)
            masked = (dy[h].astype(jnp.float32) * grad).astype(jnp.bfloat16).astype(jnp.float32) * routed
            ag_col.own(h)[...] = masked.astype(jnp.bfloat16)
            ag_col.start(h)
            ends_out[0, pl.ds(h * ROWS, ROWS), :] = value.astype(jnp.bfloat16)
        col_to_row()
        for h in halves:
            grad_hidden = rs_row.finish(h).astype(jnp.bfloat16).astype(jnp.float32)
            cross_slope(h).wait_recv()
            outgoing[h] = (grad_hidden * slope[h]).astype(jnp.bfloat16)
            cross_start(h)
        weight_grad()
        for h in halves:
            ag_col.drain(h)
            rs_row.drain(h)
            ag_row.drain(h)
            rs_col.drain(h)
            cross_drain(h)
        store_dw.wait()


def shards(ends, weights, routes):
    width = weights.shape[1]
    n = lax.axis_size("row") // 2
    half = n * ROWS
    bf16, f32 = jnp.bfloat16, jnp.float32
    dma = pltpu.SemaphoreType.DMA
    anywhere = pl.BlockSpec(memory_space=pl.ANY)
    in_vmem = pl.BlockSpec(memory_space=pltpu.VMEM)
    lines = dma((2, HALVES, n))
    line = dma((HALVES, n))
    return pl.pallas_call(
        functools.partial(kernel, n),
        out_shape=(jax.ShapeDtypeStruct(ends.shape, bf16), jax.ShapeDtypeStruct(weights.shape, bf16)),
        in_specs=[anywhere, anywhere, anywhere],
        out_specs=(in_vmem, anywhere),
        scratch_shapes=[
            pltpu.VMEM((width, width), bf16),
            pltpu.VMEM((HALVES, 2 * half, width), bf16),
            pltpu.VMEM((HALVES, 2 * half, width), bf16),
            pltpu.VMEM((HALVES, ROWS, width), bf16),
            pltpu.VMEM((HALVES, ROWS, width), bf16),
            pltpu.VMEM((HALVES, ROWS, width), f32),
            pltpu.VMEM(routes.shape, jnp.int32),
            pltpu.VMEM((2, n, 8, 128), f32),
            pltpu.VMEM((width, width), bf16),
            pltpu.VMEM((2, HALVES, 2, half, width), bf16),
            pltpu.VMEM((2, HALVES, 2, half, width), f32),
            pltpu.VMEM((2, HALVES, half, width), bf16),
            pltpu.VMEM((2, HALVES, half, width), bf16),
            pltpu.VMEM((2, HALVES, half, width), bf16),
            pltpu.VMEM((HALVES, half, width), bf16),
            lines, lines, lines, lines, lines,
            lines, lines, lines, lines, line, line,
            dma((HALVES,)), dma((HALVES,)), line, dma((HALVES,)), dma((HALVES,)),
            dma((n,)), dma((n,)), dma((1,)), dma((1,)), dma((5,)),
        ],
        compiler_params=pltpu.CompilerParams(
            collective_id=0, has_side_effects=True, vmem_limit_bytes=VMEM_LIMIT),
        cost_estimate=pl.CostEstimate(
            flops=6 * half * 4 * width * width, bytes_accessed=4 * width * width, transcendentals=0),
    )(ends, weights, routes)


def solution(mesh):
    placed = (P("section", "col", "row"), P("section", "row", "col"), P("row", None))
    return jax.shard_map(
        shards,
        mesh=mesh,
        in_specs=placed,
        out_specs=(P("section", "col", "row"), P("section", "row", "col")),
        check_vma=False,
    )
```

time: 126 us -> 113 us (0.90)
  Pallas kernels: 120 us -> 108 us
    pallas_call x1, Pallas kernels: 120 us -> 108 us  [shards(): pl.pallas_call(functools.partial(kernel, n), out_shape=(jax.ShapeDtypeStr...]
    unnamed x8 -> x2, local copies, waits for them, and re-layouts: 4.35 us -> 3.78 us
where the time goes in v2:
time: 113 us
  Pallas kernels  108 us (96%)
  local copies, waits for them, and re-layouts  3.78 us (3%)
    pallas_call x1, Pallas kernels, shards(): pl.pallas_call(functools.partial(kernel, n), out_shape=(jax.ShapeDtypeStr...  108 us
    unnamed x2, local copies, waits for them, and re-layouts  3.78 us

profile of v2, /device:TPU:1, one launch (start us, length us, event | category | flops | bytes accessed | tf_op | source)
XLA Modules:
  0.0 112.9 jit_solution(3836824717497220826)
XLA Ops:
  0.6 108.5 %shard_map.50 = (bf16[1,32,768]{2,1,0:T(8,128)(2,1)}, bf16[1,768,768]{2,1,0:T(8,128)(2,1)}) custom-call(bf16[1,32,768]{2,1,0:T(8,128)(2,1)} %ends_hbm.1, bf16[1,768,768]{2,1,0:T(8,128)(2,1)} %w_hbm.1, s32[1,16]{1,0:T(1,128)} %routes_hbm.1), custom_call_target="tpu_custom_call" | custom-call | flops 1811939328 | bytes 2359296 | tf_op jit(solution)/shard_map/pallas_call | solution.py:474
  109.1 1.4 %copy.7 = bf16[1,32,768]{2,1,0:T(8,128)(2,1)} copy(bf16[1,32,768]{2,1,0:T(8,128)(2,1)} %get-tuple-element.4) | data formatting | bytes 98304
  110.5 2.4 %copy.8 = bf16[1,768,768]{2,1,0:T(8,128)(2,1)} copy(bf16[1,768,768]{2,1,0:T(8,128)(2,1)} %get-tuple-element.5) | data formatting | bytes 2359296

commit v3 on v2

--- a/solution.py
+++ b/solution.py
@@ -9,8 +9,11 @@
 from jax.sharding import PartitionSpec as P
 
 MESH = pl.DeviceIdType.MESH
-HALVES = 2
+PARTS = 2
 ROWS = 16
+LATE_COL = 1
+LATE_ROW = 0
+LATE_SUM = 1
 TILE = 256
 FAR_GATHER = 0
 FAR_SUM = 0
@@ -29,10 +32,6 @@
     return x * cdf, cdf + 0.5 * x * (1.0 - t * t) * inner
 
 
-def rows_of(slot):
-    return pl.ds(pl.multiple_of(slot * ROWS, ROWS), ROWS)
-
-
 def over(first, last, body):
     def step(i, carry):
         body(i)
@@ -82,11 +81,11 @@
 
     def own(self, h):
         line = self.line
-        return self.buf.at[h, rows_of(line.par * line.n + line.pos)]
+        return self.buf.at[h, line.par * line.n + line.pos]
 
     def ring(self, h, block_pos, peer_pos):
         line = self.line
-        block = self.buf.at[h, rows_of(line.par * line.n + block_pos)]
+        block = self.buf.at[h, line.par * line.n + block_pos]
         return remote(block, block, self.ring_send.at[h, peer_pos], self.ring_recv.at[h, block_pos], line.peer(peer_pos))
 
     def to_ring(self, h, pos):
@@ -101,7 +100,7 @@
 
     def pair(self, h, par, pos):
         line = self.line
-        block = self.buf.at[h, rows_of(par * line.n + pos)]
+        block = self.buf.at[h, par * line.n + pos]
         return remote(block, block, self.pair_send.at[h, pos], self.pair_recv.at[h, pos], line.other(line.pos))
 
     def start(self, h):
@@ -151,11 +150,11 @@
         line = self.line
         if self.whole:
             return remote(self.out.at[h, 1 - line.par], self.got.at[h], self.pair_send.at[h, 0], self.pair_recv.at[h, 0], line.other(line.pos))
-        return remote(self.out.at[h, 1 - line.par, rows_of(pos)], self.got.at[h, rows_of(pos)],
+        return remote(self.out.at[h, 1 - line.par, pos], self.got.at[h, pos],
                       self.pair_send.at[h, pos], self.pair_recv.at[h, pos], line.other(line.pos))
 
     def ring(self, h, pos, land_pos):
-        return remote(self.both.at[h, rows_of(pos)], self.land.at[h, rows_of(land_pos)],
+        return remote(self.both.at[h, pos], self.land.at[h, land_pos],
                       self.ring_send.at[h, pos], self.ring_recv.at[h, land_pos], self.line.peer(pos))
 
     def to_ring(self, h, pos):
@@ -165,7 +164,7 @@
         return self.ring(h, pos, pos)
 
     def direct(self, h, pos, land_pos):
-        return remote(self.out.at[h, 1 - self.line.par, rows_of(pos)], self.far_land.at[h, rows_of(land_pos)],
+        return remote(self.out.at[h, 1 - self.line.par, pos], self.far_land.at[h, land_pos],
                       self.far_send.at[h, pos], self.far_recv.at[h, land_pos], self.line.other(pos))
 
     def to_far(self, h, pos):
@@ -175,21 +174,22 @@
         return self.direct(h, pos, pos)
 
     def multiply(self, h, buf, w, transposed, par):
-        size = self.line.n * ROWS
+        n = self.line.n
         width = w.shape[0]
         tile = min(TILE, width)
-        left = buf[h, pl.ds(pl.multiple_of(par * size, size), size), :]
+        left = buf[h, pl.ds(par * n, n)].reshape(n * ROWS, width)
 
         def column(j):
-            cut = pl.ds(pl.multiple_of(j * tile, tile), tile)
+            cut = pl.ds(j * tile, tile)
             if transposed:
                 value = lax.dot_general(left, w[cut, :], (((1,), (1,)), ((), ())), preferred_element_type=jnp.float32)
             else:
                 value = jnp.dot(left, w[:, cut], preferred_element_type=jnp.float32)
-            self.kept[h, par, :, cut] = value
-            self.out[h, par, :, cut] = value.astype(jnp.bfloat16)
-
-        over(0, width // tile, column)
+            self.kept[h, par, :, :, cut] = value.reshape(n, ROWS, tile)
+            self.out[h, par, :, :, cut] = value.astype(jnp.bfloat16).reshape(n, ROWS, tile)
+
+        for j in range(width // tile):
+            column(j)
 
     def send_pair(self, h):
         line = self.line
@@ -202,7 +202,7 @@
         line = self.line
 
         def send(pos):
-            self.both[h, rows_of(pos), :] = self.out[h, line.par, rows_of(pos), :]
+            self.both[h, pos, :] = self.out[h, line.par, pos, :]
             self.to_ring(h, pos).start()
 
         line.peers(0, self.far, send)
@@ -215,8 +215,8 @@
         def send(pos):
             if not self.whole:
                 self.pair(h, pos).wait_recv()
-            total = self.kept[h, line.par, rows_of(pos), :] + self.got[h, rows_of(pos), :].astype(jnp.float32)
-            self.both[h, rows_of(pos), :] = total.astype(jnp.bfloat16)
+            total = self.kept[h, line.par, pos, :] + self.got[h, pos, :].astype(jnp.float32)
+            self.both[h, pos, :] = total.astype(jnp.bfloat16)
             self.to_ring(h, pos).start()
 
         line.peers(self.far, line.n - 1, send)
@@ -225,19 +225,19 @@
         line = self.line
         if not self.whole:
             self.pair(h, line.pos).wait_recv()
-        total = self.kept[h, line.par, rows_of(line.pos), :] + self.got[h, rows_of(line.pos), :].astype(jnp.float32)
+        total = self.kept[h, line.par, line.pos, :] + self.got[h, line.pos, :].astype(jnp.float32)
 
         def near(i, total):
             pos = line.at(line.n - 2 - i)
             self.from_ring(h, pos).wait_recv()
-            return total + self.land[h, rows_of(pos), :].astype(jnp.float32)
+            return total + self.land[h, pos, :].astype(jnp.float32)
 
         total = lax.fori_loop(0, line.n - 1, near, total)
 
         def far(i, total):
             pos = line.at(self.far - 1 - i)
             self.from_far(h, pos).wait_recv()
-            return total + self.far_land[h, rows_of(pos), :].astype(jnp.float32)
+            return total + self.far_land[h, pos, :].astype(jnp.float32)
 
         return lax.fori_loop(0, self.far, far, total) if self.far else total
 
@@ -251,7 +251,7 @@
 
 
 def kernel(n, ends_hbm, w_hbm, routes_hbm, ends_out, dw_hbm,
-           w, col_buf, row_buf, dy, outgoing, slope, route_row, route_tiles, dw,
+           w, ends, col_buf, row_buf, outgoing, slope, route_row, route_tiles, dw,
            rs_out, rs_kept, rs_got, rs_both, rs_land, rs_far_land,
            ag_ring_send, ag_ring_recv, ag_pair_send, ag_pair_recv, ag_far_send,
            rs_ring_send, rs_ring_recv, rs_pair_send, rs_pair_recv, rs_far_send, rs_far_recv,
@@ -262,7 +262,7 @@
     col = Line("col", n, lambda i: (s, r, i))
     over_there = (1 - s, r, c)
     far_gather, far_sum, far_cross = (min(far, n - 1) for far in (FAR_GATHER, FAR_SUM, FAR_CROSS))
-    halves = range(HALVES)
+    parts = range(PARTS)
 
     def gather(line, buf, skip, far, k):
         return Gather(line, buf, skip, far, ag_ring_send.at[k], ag_ring_recv.at[k],
@@ -298,10 +298,12 @@
 
     load_w = pltpu.make_async_copy(w_hbm.at[0], w, local_sem.at[0])
     store_dw = pltpu.make_async_copy(dw, dw_hbm.at[0], local_sem.at[1])
-    load_routes = pltpu.make_async_copy(routes_hbm, route_row, local_sem.at[4])
-
-    def load_ends(h, dst):
-        return pltpu.make_async_copy(ends_hbm.at[0, pl.ds(h * ROWS, ROWS)], dst, local_sem.at[2 + h])
+    load_routes = pltpu.make_async_copy(routes_hbm, route_row, local_sem.at[3])
+
+    load_ends = pltpu.make_async_copy(ends_hbm.at[0], ends, local_sem.at[2])
+
+    def ends_part(h):
+        return ends[pl.ds(h * ROWS, ROWS), :]
 
     barrier = pltpu.get_barrier_semaphore()
 
@@ -326,9 +328,10 @@
             at_row = pl.ds(pl.multiple_of((k // (width // tile)) * tile, tile), tile)
             at_col = pl.ds(pl.multiple_of((k % (width // tile)) * tile, tile), tile)
             total = jnp.zeros((tile, tile), jnp.float32)
-            for h in halves:
+            for h in parts:
                 total = total + lax.dot_general(
-                    col_buf[h, :, at_row], row_buf[h, :, at_col], (((0,), (0,)), ((), ())),
+                    col_buf[h, :, :, at_row].reshape(-1, tile), row_buf[h, :, :, at_col].reshape(-1, tile),
+                    (((0,), (0,)), ((), ())),
                     preferred_element_type=jnp.float32)
             dw[at_row, at_col] = total.astype(jnp.bfloat16)
 
@@ -338,65 +341,83 @@
     same = row.par == col.par
     differ = row.par != col.par
 
+    def staggered(early, late, lag):
+        for h in range(PARTS + lag):
+            if h < PARTS:
+                early(h)
+            if h >= lag:
+                late(h - lag)
+
     def col_to_row():
-        for h in halves:
+        def early(h):
             ag_col.finish_ring(h)
             if h == 0:
                 pl.when(s == 0)(load_w.wait)
             rs_row.multiply(h, col_buf, w, False, col.par)
             pl.when(differ)(lambda: rs_row.send_pair(h))
             pl.when(same)(lambda: rs_row.combine(h))
-        for h in halves:
+
+        def late(h):
             ag_col.finish_pair(h)
             rs_row.multiply(h, col_buf, w, False, 1 - col.par)
             pl.when(same)(lambda: rs_row.send_pair(h))
             pl.when(differ)(lambda: rs_row.combine(h))
 
+        staggered(early, late, LATE_COL)
+
     def row_to_col():
-        for h in halves:
+        def early(h):
             ag_row.finish_ring(h)
             if h == 0:
                 pl.when(s == 1)(load_w.wait)
             rs_col.multiply(h, row_buf, w, True, row.par)
             pl.when(differ)(lambda: rs_col.send_pair(h))
             pl.when(same)(lambda: rs_col.send_far(h))
+
+        def late(h):
             ag_row.finish_pair(h)
             rs_col.multiply(h, row_buf, w, True, 1 - row.par)
             pl.when(same)(lambda: rs_col.send_pair(h))
             pl.when(differ)(lambda: rs_col.send_far(h))
-        for h in halves:
-            rs_col.combine(h)
+
+        for h in range(PARTS + max(LATE_ROW, LATE_SUM)):
+            if h < PARTS:
+                early(h)
+            if 0 <= h - LATE_SUM < PARTS:
+                rs_col.combine(h - LATE_SUM)
+            if 0 <= h - LATE_ROW < PARTS:
+                late(h - LATE_ROW)
 
     @pl.when(s == 0)
     def _():
-        for h in halves:
-            load_ends(h, ag_col.own(h)).start()
+        load_ends.start()
         load_w.start()
-        for h in halves:
-            load_ends(h, ag_col.own(h)).wait()
+        load_ends.wait()
+        for h in parts:
+            ag_col.own(h)[...] = ends_part(h)
         pl.semaphore_wait(barrier, greetings)
-        for h in halves:
+        for h in parts:
             ag_col.start(h)
         col_to_row()
-        for h in halves:
+        for h in parts:
             value, grad = gelu_pair(rs_row.finish(h))
             outgoing[h] = value.astype(jnp.bfloat16)
             cross_start(h)
             slope[h] = grad
             cross_slope(h).start()
-        for h in halves:
+        for h in parts:
             ag_col.drain(h)
             rs_row.drain(h)
             cross_drain(h)
             cross_slope(h).wait_send()
-        for h in halves:
+        for h in parts:
             cross(h).wait_recv()
             ag_row.start(h)
         row_to_col()
         weight_grad()
-        for h in halves:
+        for h in parts:
             ends_out[0, pl.ds(h * ROWS, ROWS), :] = rs_col.finish(h).astype(jnp.bfloat16)
-        for h in halves:
+        for h in parts:
             ag_row.drain(h)
             rs_col.drain(h)
         store_dw.wait()
@@ -404,14 +425,12 @@
     @pl.when(s == 1)
     def _():
         load_routes.start()
-        for h in halves:
-            load_ends(h, dy.at[h]).start()
+        load_ends.start()
         load_w.start()
         load_routes.wait()
         route_tiles[row.par, row.pos] = jnp.zeros((8, 128), jnp.float32)
         route_tiles[row.par, row.pos, 0:1, 0:2 * n] = route_row[...].astype(jnp.float32)
-        for h in halves:
-            load_ends(h, dy.at[h]).wait()
+        load_ends.wait()
         pl.semaphore_wait(barrier, greetings)
 
         def tile_to(pos):
@@ -435,24 +454,24 @@
         lanes = lax.broadcasted_iota(jnp.int32, (1, 128), 1)
         routed = jnp.sum(jnp.where(lanes == r, picked, 0.0), axis=1, keepdims=True)
 
-        for h in halves:
+        for h in parts:
             cross(h).wait_recv()
             ag_row.start(h)
         row_to_col()
-        for h in halves:
+        for h in parts:
             value, grad = gelu_pair(rs_col.finish(h) * routed)
-            masked = (dy[h].astype(jnp.float32) * grad).astype(jnp.bfloat16).astype(jnp.float32) * routed
+            masked = (ends_part(h).astype(jnp.float32) * grad).astype(jnp.bfloat16).astype(jnp.float32) * routed
             ag_col.own(h)[...] = masked.astype(jnp.bfloat16)
             ag_col.start(h)
             ends_out[0, pl.ds(h * ROWS, ROWS), :] = value.astype(jnp.bfloat16)
         col_to_row()
-        for h in halves:
+        for h in parts:
             grad_hidden = rs_row.finish(h).astype(jnp.bfloat16).astype(jnp.float32)
             cross_slope(h).wait_recv()
             outgoing[h] = (grad_hidden * slope[h]).astype(jnp.bfloat16)
             cross_start(h)
         weight_grad()
-        for h in halves:
+        for h in parts:
             ag_col.drain(h)
             rs_row.drain(h)
             ag_row.drain(h)
@@ -464,13 +483,12 @@
 def shards(ends, weights, routes):
     width = weights.shape[1]
     n = lax.axis_size("row") // 2
-    half = n * ROWS
     bf16, f32 = jnp.bfloat16, jnp.float32
     dma = pltpu.SemaphoreType.DMA
     anywhere = pl.BlockSpec(memory_space=pl.ANY)
     in_vmem = pl.BlockSpec(memory_space=pltpu.VMEM)
-    lines = dma((2, HALVES, n))
-    line = dma((HALVES, n))
+    lines = dma((2, PARTS, n))
+    line = dma((PARTS, n))
     return pl.pallas_call(
         functools.partial(kernel, n),
         out_shape=(jax.ShapeDtypeStruct(ends.shape, bf16), jax.ShapeDtypeStruct(weights.shape, bf16)),
@@ -478,29 +496,29 @@
         out_specs=(in_vmem, anywhere),
         scratch_shapes=[
             pltpu.VMEM((width, width), bf16),
-            pltpu.VMEM((HALVES, 2 * half, width), bf16),
-            pltpu.VMEM((HALVES, 2 * half, width), bf16),
-            pltpu.VMEM((HALVES, ROWS, width), bf16),
-            pltpu.VMEM((HALVES, ROWS, width), bf16),
-            pltpu.VMEM((HALVES, ROWS, width), f32),
+            pltpu.VMEM(ends.shape[1:], bf16),
+            pltpu.VMEM((PARTS, 2 * n, ROWS, width), bf16),
+            pltpu.VMEM((PARTS, 2 * n, ROWS, width), bf16),
+            pltpu.VMEM((PARTS, ROWS, width), bf16),
+            pltpu.VMEM((PARTS, ROWS, width), f32),
             pltpu.VMEM(routes.shape, jnp.int32),
             pltpu.VMEM((2, n, 8, 128), f32),
             pltpu.VMEM((width, width), bf16),
-            pltpu.VMEM((2, HALVES, 2, half, width), bf16),
-            pltpu.VMEM((2, HALVES, 2, half, width), f32),
-            pltpu.VMEM((2, HALVES, half, width), bf16),
-            pltpu.VMEM((2, HALVES, half, width), bf16),
-            pltpu.VMEM((2, HALVES, half, width), bf16),
-            pltpu.VMEM((HALVES, half, width), bf16),
+            pltpu.VMEM((2, PARTS, 2, n, ROWS, width), bf16),
+            pltpu.VMEM((2, PARTS, 2, n, ROWS, width), f32),
+            pltpu.VMEM((2, PARTS, n, ROWS, width), bf16),
+            pltpu.VMEM((2, PARTS, n, ROWS, width), bf16),
+            pltpu.VMEM((2, PARTS, n, ROWS, width), bf16),
+            pltpu.VMEM((PARTS, n, ROWS, width), bf16),
             lines, lines, lines, lines, lines,
             lines, lines, lines, lines, line, line,
-            dma((HALVES,)), dma((HALVES,)), line, dma((HALVES,)), dma((HALVES,)),
-            dma((n,)), dma((n,)), dma((1,)), dma((1,)), dma((5,)),
+            dma((PARTS,)), dma((PARTS,)), line, dma((PARTS,)), dma((PARTS,)),
+            dma((n,)), dma((n,)), dma((1,)), dma((1,)), dma((4,)),
         ],
         compiler_params=pltpu.CompilerParams(
             collective_id=0, has_side_effects=True, vmem_limit_bytes=VMEM_LIMIT),
         cost_estimate=pl.CostEstimate(
-            flops=6 * half * 4 * width * width, bytes_accessed=4 * width * width, transcendentals=0),
+            flops=24 * n * PARTS * ROWS * width * width, bytes_accessed=4 * width * width, transcendentals=0),
     )(ends, weights, routes)
 
 

time: 113 us -> 110 us (0.973)
  Pallas kernels: 108 us -> 106 us
    pallas_call x1, Pallas kernels: 108 us -> 106 us  [shards(): pl.pallas_call(functools.partial(kernel, n), out_shape=(jax.ShapeDtypeStr...]
where the time goes in v3:
time: 110 us
  Pallas kernels  106 us (96%)
  local copies, waits for them, and re-layouts  3.78 us (3%)
    pallas_call x1, Pallas kernels, shards(): pl.pallas_call(functools.partial(kernel, n), out_shape=(jax.ShapeDtypeStr...  106 us
    unnamed x2, local copies, waits for them, and re-layouts  3.78 us

profile of v3, /device:TPU:1, one launch (start us, length us, event | category | flops | bytes accessed | tf_op | source)
XLA Modules:
  0.0 110.0 jit_solution(6295413971293777904)
XLA Ops:
  0.6 105.6 %shard_map.50 = (bf16[1,32,768]{2,1,0:T(8,128)(2,1)}, bf16[1,768,768]{2,1,0:T(8,128)(2,1)}) custom-call(bf16[1,32,768]{2,1,0:T(8,128)(2,1)} %ends_hbm.1, bf16[1,768,768]{2,1,0:T(8,128)(2,1)} %w_hbm.1, s32[1,16]{1,0:T(1,128)} %routes_hbm.1), custom_call_target="tpu_custom_call" | custom-call | flops 3623878656 | bytes 2359296 | tf_op jit(solution)/shard_map/pallas_call | solution.py:492
  106.3 1.4 %copy.7 = bf16[1,32,768]{2,1,0:T(8,128)(2,1)} copy(bf16[1,32,768]{2,1,0:T(8,128)(2,1)} %get-tuple-element.4) | data formatting | bytes 98304
  107.7 2.4 %copy.8 = bf16[1,768,768]{2,1,0:T(8,128)(2,1)} copy(bf16[1,768,768]{2,1,0:T(8,128)(2,1)} %get-tuple-element.5) | data formatting | bytes 2359296

commit v4 on v3

--- a/solution.py
+++ b/solution.py
@@ -38,7 +38,7 @@
         return carry
 
     if first < last:
-        lax.fori_loop(first, last, step, 0)
+        lax.fori_loop(first, last, step, 0, unroll=last - first < 9)
 
 
 def remote(src, dst, send_sem, recv_sem, device):
@@ -232,7 +232,7 @@
             self.from_ring(h, pos).wait_recv()
             return total + self.land[h, pos, :].astype(jnp.float32)
 
-        total = lax.fori_loop(0, line.n - 1, near, total)
+        total = lax.fori_loop(0, line.n - 1, near, total, unroll=True)
 
         def far(i, total):
             pos = line.at(self.far - 1 - i)

time: 110 us -> 109 us (level)
  Pallas kernels: 106 us -> 104 us
    pallas_call x1, Pallas kernels: 106 us -> 104 us  [shards(): pl.pallas_call(functools.partial(kernel, n), out_shape=(jax.ShapeDtypeStr...]
where the time goes in v4:
time: 109 us
  Pallas kernels  104 us (95%)
  local copies, waits for them, and re-layouts  3.78 us (3%)
    pallas_call x1, Pallas kernels, shards(): pl.pallas_call(functools.partial(kernel, n), out_shape=(jax.ShapeDtypeStr...  104 us
    unnamed x2, local copies, waits for them, and re-layouts  3.78 us

profile of v4, /device:TPU:1, one launch (start us, length us, event | category | flops | bytes accessed | tf_op | source)
XLA Modules:
  0.0 108.9 jit_solution(15651716738687115463)
XLA Ops:
  0.6 104.5 %shard_map.50 = (bf16[1,32,768]{2,1,0:T(8,128)(2,1)}, bf16[1,768,768]{2,1,0:T(8,128)(2,1)}) custom-call(bf16[1,32,768]{2,1,0:T(8,128)(2,1)} %ends_hbm.1, bf16[1,768,768]{2,1,0:T(8,128)(2,1)} %w_hbm.1, s32[1,16]{1,0:T(1,128)} %routes_hbm.1), custom_call_target="tpu_custom_call" | custom-call | flops 3623878656 | bytes 2359296 | tf_op jit(solution)/shard_map/pallas_call | solution.py:492
  105.1 1.4 %copy.7 = bf16[1,32,768]{2,1,0:T(8,128)(2,1)} copy(bf16[1,32,768]{2,1,0:T(8,128)(2,1)} %get-tuple-element.4) | data formatting | bytes 98304
  106.6 2.4 %copy.8 = bf16[1,768,768]{2,1,0:T(8,128)(2,1)} copy(bf16[1,768,768]{2,1,0:T(8,128)(2,1)} %get-tuple-element.5) | data formatting | bytes 2359296

commit v5 on v4

--- a/solution.py
+++ b/solution.py
@@ -416,11 +416,11 @@
         row_to_col()
         weight_grad()
         for h in parts:
-            ends_out[0, pl.ds(h * ROWS, ROWS), :] = rs_col.finish(h).astype(jnp.bfloat16)
-        for h in parts:
             ag_row.drain(h)
             rs_col.drain(h)
         store_dw.wait()
+        for h in parts:
+            ends_out[0, pl.ds(h * ROWS, ROWS), :] = rs_col.finish(h).astype(jnp.bfloat16)
 
     @pl.when(s == 1)
     def _():

time: 109 us -> 109 us (level)
  no operation moved by 1% of the time
where the time goes in v5:
time: 109 us
  Pallas kernels  104 us (95%)
  local copies, waits for them, and re-layouts  3.78 us (3%)
    pallas_call x1, Pallas kernels, shards(): pl.pallas_call(functools.partial(kernel, n), out_shape=(jax.ShapeDtypeStr...  104 us
    unnamed x2, local copies, waits for them, and re-layouts  3.78 us

profile of v5, /device:TPU:1, one launch (start us, length us, event | category | flops | bytes accessed | tf_op | source)
XLA Modules:
  0.0 108.8 jit_solution(16333404060576709053)
XLA Ops:
  0.6 104.4 %shard_map.50 = (bf16[1,32,768]{2,1,0:T(8,128)(2,1)}, bf16[1,768,768]{2,1,0:T(8,128)(2,1)}) custom-call(bf16[1,32,768]{2,1,0:T(8,128)(2,1)} %ends_hbm.1, bf16[1,768,768]{2,1,0:T(8,128)(2,1)} %w_hbm.1, s32[1,16]{1,0:T(1,128)} %routes_hbm.1), custom_call_target="tpu_custom_call" | custom-call | flops 3623878656 | bytes 2359296 | tf_op jit(solution)/shard_map/pallas_call | solution.py:492
  105.0 1.4 %copy.7 = bf16[1,32,768]{2,1,0:T(8,128)(2,1)} copy(bf16[1,32,768]{2,1,0:T(8,128)(2,1)} %get-tuple-element.4) | data formatting | bytes 98304
  106.5 2.4 %copy.8 = bf16[1,768,768]{2,1,0:T(8,128)(2,1)} copy(bf16[1,768,768]{2,1,0:T(8,128)(2,1)} %get-tuple-element.5) | data formatting | bytes 2359296
